TPU v7x, 256 devices: a whole 4x4x8 slice. The times are simulated.
256 devices in a mesh: blk: 8 (over y, core), req: 32 (over z, x).
Axes of the slice: x: 4, y: 4, z: 8, core: 2. Of those that a mesh axis runs over, the one named last changes fastest.
Arguments:
- hidden: bfloat16 [12288, 8192], P('req', 'blk'), may hold values from -120 to 120
- input_norm_gain: float32 [8192], replicated, may hold values from 0.1 to 1.9
- query_weight: bfloat16 [8192, 8192], P('req', 'blk')
- keyvalue_weight: bfloat16 [8192, 2048], P('req', 'blk')
- adapter_down: bfloat16 [32, 3, 16, 8192], P('req', None, None, 'blk'), may hold values from -0.0625 to 0.0625
- adapter_up_query: bfloat16 [32, 16, 8192], P('req', None, 'blk'), may hold values from -1.5 to 1.5
- adapter_up_keyvalue: bfloat16 [32, 16, 2048], P('req', None, 'blk'), may hold values from -1.5 to 1.5
- packed_lengths: int32 [32, 4], P('req'), may hold values from 1 to 192, 384 in all within a row
- prompt_adapter: int32 [32, 4], P('req'), may hold values from 0 to 31
Outputs:
- context: bfloat16 [12288, 8192], P('req', 'blk')
- key_cache: bfloat16 [12288, 1024], P('req', 'blk')
- value_cache: bfloat16 [12288, 1024], P('req', 'blk')
Inputs may be any that keep to these rules, and one draw needn't show every extreme that they name: `packed_lengths`: each row sums to 384; the longest prompt of the whole draw has 192 tokens.
All inputs are finite; a program needn't handle non-finite values.
Results may differ from a plain program's by a relative error of at most 0.012.
The roundings to bfloat16 on the way count: a program that leaves them out, or rounds other values in their place, can miss the bound.
Values may be sent and summed in bfloat16 or wider, within the bound.
A program may use at most 128 MiB of HBM per device.

v0:
```python
import math

import jax
import jax.numpy as jnp
from jax import lax
from jax.sharding import PartitionSpec as P

HEAD_WIDTH = 128
QUERY_LOCAL = 8
KEYVALUE_LOCAL = 1


epsilon = 1e-05
adapter_scale = 2.0
rope_base = 10000.0


def apply_rotation(vectors, cosine_table, sine_table):
    half_size = vectors.shape[-1] // 2
    first_half = vectors[..., :half_size]
    second_half = vectors[..., half_size:]
    turned = jnp.concatenate([-second_half, first_half], axis=-1)
    return vectors * cosine_table + turned * sine_table


def layout(lengths, count):
    slot_index = jnp.arange(count, dtype=jnp.int32)
    prompt_ends = jnp.cumsum(lengths)
    prompt_starts = prompt_ends - lengths
    member = (slot_index[:, None] >= prompt_starts[None, :]) & (
        slot_index[:, None] < prompt_ends[None, :]
    )
    position = jnp.sum(jnp.where(member, slot_index[:, None] - prompt_starts[None, :], 0), axis=1)
    owner = jnp.sum((slot_index[:, None] >= prompt_ends[None, :]).astype(jnp.int32), axis=1)
    return (member.astype(jnp.float32), position, owner, slot_index)


def rope_tables(position, head_size):
    frequency = rope_base ** (-(jnp.arange(head_size // 2, dtype=jnp.float32) * 2.0 / head_size))
    angles = position.astype(jnp.float32)[:, None] * frequency[None, :]
    cosine_table = jnp.cos(angles)
    sine_table = jnp.sin(angles)
    return (
        jnp.concatenate([cosine_table, cosine_table], 1)[:, None, :],
        jnp.concatenate([sine_table, sine_table], 1)[:, None, :],
    )


def shards(
    hidden,
    input_norm_gain,
    query_weight,
    keyvalue_weight,
    adapter_down,
    adapter_up_query,
    adapter_up_keyvalue,
    packed_lengths,
    prompt_adapter,
):
    row_number, feature_cols = hidden.shape
    full_width = feature_cols * lax.axis_size("blk")
    offset = lax.axis_index("blk") * feature_cols
    values = hidden.astype(jnp.float32)
    gain_part = lax.dynamic_slice_in_dim(input_norm_gain, offset, feature_cols, 0)
    squares = lax.psum(jnp.sum(values * values, axis=1), "blk")
    factor = lax.rsqrt(squares / full_width + epsilon)
    normed_part = (values * factor[:, None] * gain_part[None, :]).astype(jnp.bfloat16)
    normed = lax.all_gather(normed_part, "blk", axis=1, tiled=True)
    query_cols = query_weight.shape[1]

    def add_rows(weight_piece):
        return jnp.dot(normed, weight_piece, preferred_element_type=jnp.float32)

    query_plain = add_rows(lax.all_gather(query_weight, "req", axis=0, tiled=True))
    base_pair = add_rows(lax.all_gather(keyvalue_weight, "req", axis=0, tiled=True))
    down_all, up_query_all, up_pair_all = (
        lax.all_gather(adapter_down, "req", axis=0, tiled=True),
        lax.all_gather(adapter_up_query, "req", axis=0, tiled=True),
        lax.all_gather(adapter_up_keyvalue, "req", axis=0, tiled=True),
    )
    adapter_count = down_all.shape[0]
    lengths = packed_lengths[0]
    member, position, owner, slot_index = layout(lengths, row_number)
    prompt_count = lengths.shape[0]
    picked_adapter = (
        prompt_adapter[0][:, None] == jnp.arange(adapter_count, dtype=jnp.int32)[None, :]
    ).astype(jnp.bfloat16)
    down_selected = jnp.einsum(
        "pa,ajrd->pjrd", picked_adapter, down_all, preferred_element_type=jnp.float32
    ).astype(jnp.bfloat16)
    rank_size = down_selected.shape[2]
    partial_value = lax.dot_general(
        normed_part,
        down_selected.reshape(prompt_count * 3 * rank_size, feature_cols),
        (((1,), (1,)), ((), ())),
        preferred_element_type=jnp.float32,
    )
    partial_value = partial_value.reshape(row_number, prompt_count, 3, rank_size)
    masked = jnp.sum(partial_value * member[:, :, None, None], axis=1).reshape(
        row_number, 3 * rank_size
    )
    low_rank = lax.psum(masked, "blk").reshape(row_number, 3, rank_size).astype(jnp.bfloat16)
    low_float = low_rank.astype(jnp.float32)

    def spread(column):
        return (
            (member[:, :, None] * low_float[:, None, column, :])
            .astype(jnp.bfloat16)
            .reshape(row_number, prompt_count * rank_size)
        )

    up_query_selected = jnp.einsum(
        "pa,arc->prc", picked_adapter, up_query_all, preferred_element_type=jnp.float32
    ).astype(jnp.bfloat16)
    up_keyvalue_selected = jnp.einsum(
        "pa,arc->prc", picked_adapter, up_pair_all, preferred_element_type=jnp.float32
    ).astype(jnp.bfloat16)
    up_keyvalue_selected = up_keyvalue_selected.reshape(
        prompt_count, rank_size, KEYVALUE_LOCAL, 2, HEAD_WIDTH
    )
    query_update = jnp.dot(
        spread(0),
        up_query_selected.reshape(prompt_count * rank_size, query_cols),
        preferred_element_type=jnp.float32,
    )
    key_update = jnp.dot(
        spread(1),
        up_keyvalue_selected[:, :, :, 0].reshape(
            prompt_count * rank_size, KEYVALUE_LOCAL * HEAD_WIDTH
        ),
        preferred_element_type=jnp.float32,
    )
    value_update = jnp.dot(
        spread(2),
        up_keyvalue_selected[:, :, :, 1].reshape(
            prompt_count * rank_size, KEYVALUE_LOCAL * HEAD_WIDTH
        ),
        preferred_element_type=jnp.float32,
    )
    cosine_table, sine_table = rope_tables(position, HEAD_WIDTH)
    query_complete = (query_plain + adapter_scale * query_update).reshape(
        row_number, QUERY_LOCAL * KEYVALUE_LOCAL, HEAD_WIDTH
    )
    query_states = apply_rotation(query_complete, cosine_table, sine_table).astype(jnp.bfloat16)
    keyvalue_plain = base_pair.reshape(row_number, KEYVALUE_LOCAL, 2, HEAD_WIDTH)
    key_vectors = apply_rotation(
        keyvalue_plain[:, :, 0]
        + adapter_scale * key_update.reshape(row_number, KEYVALUE_LOCAL, HEAD_WIDTH),
        cosine_table,
        sine_table,
    ).astype(jnp.bfloat16)
    value_vectors = (
        keyvalue_plain[:, :, 1]
        + adapter_scale * value_update.reshape(row_number, KEYVALUE_LOCAL, HEAD_WIDTH)
    ).astype(jnp.bfloat16)
    grouped = query_states.reshape(row_number, KEYVALUE_LOCAL, QUERY_LOCAL, HEAD_WIDTH)
    scores = jnp.einsum(
        "tkgc,skc->kgts", grouped, key_vectors, preferred_element_type=jnp.float32
    ) / math.sqrt(HEAD_WIDTH)
    allowed = (owner[:, None] == owner[None, :]) & (slot_index[None, :] <= slot_index[:, None])
    scores = jnp.where(allowed[None, None], scores, -1e30)
    row_max = jnp.max(scores, axis=-1, keepdims=True)
    exponent = jnp.exp(scores - row_max)
    attend = (exponent / jnp.sum(exponent, axis=-1, keepdims=True)).astype(jnp.bfloat16)
    context = jnp.einsum(
        "kgts,skc->tkgc", attend, value_vectors, preferred_element_type=jnp.float32
    ).astype(jnp.bfloat16)
    return (
        context.reshape(row_number, KEYVALUE_LOCAL * QUERY_LOCAL * HEAD_WIDTH),
        key_vectors.reshape(row_number, KEYVALUE_LOCAL * HEAD_WIDTH),
        value_vectors.reshape(row_number, KEYVALUE_LOCAL * HEAD_WIDTH),
    )


def solution(mesh):
    in_specs = (
        P("req", "blk"),
        P(),
        P("req", "blk"),
        P("req", "blk"),
        P("req", None, None, "blk"),
        P("req", None, "blk"),
        P("req", None, "blk"),
        P("req", None),
        P("req", None),
    )
    out_specs = (P("req", "blk"), P("req", "blk"), P("req", "blk"))
    return jax.shard_map(shards, mesh=mesh, in_specs=in_specs, out_specs=out_specs, check_vma=False)
```

profile of v0, /device:TPU:6, one launch (start us, length us, event | category | flops | bytes accessed | tf_op | source)
XLA Modules:
  0.0 460.6 jit_solution(1548275453089813098)
XLA Ops:
  7.2 0.0 copy-start
  7.2 0.0 all-gather.14.cloned.1.call-start
  7.2 0.7 all-gather.14.cloned.1.call-update
  7.9 0.0 all-gather.10.cloned.1.call-start
  8.0 0.7 all-gather.10.cloned.1.call-update
  8.7 0.0 all-gather.8.cloned.1.call-start
  8.7 0.7 all-gather.8.cloned.1.call-update
  9.4 0.0 all-gather.6.cloned.1.call-start
  9.4 0.7 dynamic_slice.3
  10.1 1.4 fusion.7
  11.5 0.0 copy-start.6
  11.5 0.0 copy-start.4
  11.5 14.9 %psum.14 = f32[384]{0:T(512)S(1)} all-reduce(f32[384]{0:T(512)S(1)} %fusion.7), channel_id=1, replica_groups=mesh['blk'=8,'req'=32] {'blk'}, use_global_device_ids=true, to_apply=%region_1.0 | all-reduce | flops 384 | bytes 3072 | tf_op jit(solution)/shard_map/psum | solution.py:65
  26.4 0.0 copy-done
  26.4 0.0 copy-start.5
  26.4 1.1 fusion.9
  27.5 0.0 all-gather.6.cloned.1.call-update
  27.6 0.0 all-gather.12.cloned.1.call-start
  27.6 0.5 all-gather.12.cloned.1.call-update
  28.1 0.0 copy-done.6
  28.2 0.2 reduce-window.4
  28.3 0.0 copy-done.4
  28.3 51.7 %all_gather.21 = bf16[32,16,256]{2,1,0:T(8,128)(2,1)S(1)} all-gather(bf16[1,16,256]{2,1,0:T(8,128)(2,1)S(1)} %copy-done.4), channel_id=1, replica_groups=mesh['blk'=8,'req'=32] {'req'}, dimensions={0}, use_global_device_ids=true | all-gather | bytes 270336 | tf_op jit(solution)/shard_map/all_gather | solution.py:79
  80.1 0.0 copy-done.5
  80.1 0.2 convolution_convert_fusion.1
  80.3 0.1 fusion.54
  80.4 0.1 convert_reduce_fusion
  80.5 0.1 fusion.52
  80.6 0.1 fusion.28
  80.7 0.8 multiply_cosine_fusion
  81.5 7.2 %all-gather.14.cloned.1.call-done = bf16[32,16,1024]{2,1,0:T(8,128)(2,1)} async-done(((bf16[1,16,1024]{2,1,0:T(8,128)(2,1)}), bf16[32,16,1024]{2,1,0:T(8,128)(2,1)}) %all-gather.14.cloned.1.call-update) | async-done | bytes 1048592 | tf_op jit(solution)/shard_map/all_gather | solution.py:78
  88.7 2.4 convolution_convert_fusion
  91.2 0.0 copy-start.1
  91.2 77.2 %all-gather.10.cloned.1.call-done = bf16[32,3,16,1024]{3,2,1,0:T(8,128)(2,1)} async-done(((bf16[1,3,16,1024]{3,2,1,0:T(8,128)(2,1)}), bf16[32,3,16,1024]{3,2,1,0:T(8,128)(2,1)}) %all-gather.10.cloned.1.call-update) | async-done | bytes 3145744 | tf_op jit(solution)/shard_map/all_gather | solution.py:77
  168.3 5.4 %fusion.15 = bf16[4,3,16,1024]{3,0,2,1:T(4,128)(2,1)S(1)} fusion(bf16[32,3,16,1024]{3,2,1,0:T(8,128)(2,1)} %all-gather.10.cloned.1.call-done, s32[4]{0:T(128)S(1)} %bitcast.137), kind=kOutput, calls=%fused_computation.23 | convolution fusion | flops 12779648 | bytes 3538960 | tf_op jit(solution)/shard_map/pa,ajrd->pjrd/dot_general | solution.py:88
  173.7 0.0 copy-done.1
  173.7 0.5 fusion.20
  174.1 24.9 %psum.15 = bf16[384,48]{0,1:T(8,128)(2,1)S(1)} all-reduce(f32[384,48]{0,1:T(8,128)S(1)} %bitcast.132), channel_id=1, replica_groups=mesh['blk'=8,'req'=32] {'blk'}, use_global_device_ids=true, to_apply=%region_4.5 | all-reduce | flops 18432 | bytes 110592 | tf_op jit(solution)/shard_map/psum | solution.py:102
  199.2 0.4 fusion.34
  199.5 49.5 %all-gather.8.cloned.1.call-done = bf16[8192,256]{1,0:T(8,128)(2,1)} async-done(((bf16[256,256]{1,0:T(8,128)(2,1)}), bf16[8192,256]{1,0:T(8,128)(2,1)}) %all-gather.8.cloned.1.call-update) | async-done | bytes 4194320 | tf_op jit(solution)/shard_map/all_gather | solution.py:75
  249.0 45.0 %all-gather.6.cloned.1.call-done = bf16[384,8192]{1,0:T(8,128)(2,1)} async-done(((bf16[384,1024]{1,0:T(8,128)(2,1)}), bf16[384,8192]{1,0:T(8,128)(2,1)}) %all-gather.6.cloned.1.call-update) | async-done | bytes 6291472 | tf_op jit(solution)/shard_map/all_gather | solution.py:68
  294.0 6.4 %fusion.55 = f32[384,256]{0,1:T(8,128)S(1)} fusion(bf16[384,8192]{1,0:T(8,128)(2,1)} %all-gather.6.cloned.1.call-done, bf16[8192,256]{1,0:T(8,128)(2,1)} %all-gather.8.cloned.1.call-done), kind=kOutput, calls=%fused_computation.86 | convolution fusion | flops 1610612736 | bytes 10878976 | tf_op jit(solution)/shard_map/dot_general | solution.py:72
  300.5 0.1 copy.52
  300.6 0.1 copy.50
  300.7 0.2 fusion.21
  301.0 0.0 copy-start.3
  301.0 0.2 fusion.18
  301.2 0.1 fusion.31
  301.3 0.2 fusion.33
  301.5 0.0 copy-start.2
  301.6 133.7 %all-gather.12.cloned.1.call-done = bf16[8192,1024]{1,0:T(8,128)(2,1)} async-done(((bf16[256,1024]{1,0:T(8,128)(2,1)}), bf16[8192,1024]{1,0:T(8,128)(2,1)}) %all-gather.12.cloned.1.call-update) | async-done | bytes 16777232 | tf_op jit(solution)/shard_map/all_gather | solution.py:74
  435.3 12.0 %fusion.11 = f32[384,1024]{1,0:T(8,128)S(1)} fusion(f32[384,1024,1]{1,0,2:T(8,128)S(1)} %fusion.34, bf16[384,8192]{1,0:T(8,128)(2,1)} %all-gather.6.cloned.1.call-done, bf16[8192,1024]{1,0:T(8,128)(2,1)} %all-gather.12.cloned.1.call-done), kind=kOutput, calls=%fused_computation.21 | convolution fusion | flops 6443237376 | bytes 26214400 | tf_op jit(solution)/shard_map/dot_general | solution.py:72
  447.3 0.3 copy.56
  447.7 0.5 slice_negate_fusion
  448.2 0.6 maximum_multiply_fusion
  448.7 0.1 mul.179
  448.9 0.0 copy-done.2
  448.9 1.4 fusion.1
  450.3 1.0 fusion
  451.3 0.0 copy-done.3
  451.3 1.6 fusion.12
  452.9 1.2 copy.43
  (11 shorter events, 0.1 us)
Async XLA Ops:
  7.2 19.2 %copy-start = (bf16[384,1024]{1,0:T(8,128)(2,1)S(1)}, bf16[384,1024]{1,0:T(8,128)(2,1)}, u32[]{:S(2)}) copy-start(bf16[384,1024]{1,0:T(8,128)(2,1)} %param.9) | copy-start | bytes 2359300
  7.2 81.5 %all-gather.14.cloned.1.call-start = ((), (), s32[]{:S(2)}) async-start(), calls=%async_computation.4 | async-start | bytes 1081344 | tf_op jit(solution)/shard_map/all_gather | solution.py:78
  7.9 160.4 %all-gather.10.cloned.1.call-start = ((), (), s32[]{:S(2)}) async-start(), calls=%async_computation.2 | async-start | bytes 3244032 | tf_op jit(solution)/shard_map/all_gather | solution.py:77
  8.7 240.4 %all-gather.8.cloned.1.call-start = ((), (), s32[]{:S(2)}) async-start(), calls=%async_computation.1 | async-start | bytes 4325376 | tf_op jit(solution)/shard_map/all_gather | solution.py:75
  9.4 284.7 %all-gather.6.cloned.1.call-start = ((), (), s32[]{:S(2)}) async-start(), calls=%async_computation | async-start | bytes 7077888 | tf_op jit(solution)/shard_map/all_gather | solution.py:68
  11.5 16.6 %copy-start.6 = (s32[1,4]{1,0:T(1,128)S(1)}, s32[1,4]{1,0:T(1,128)}, u32[]{:S(2)}) copy-start(s32[1,4]{1,0:T(1,128)} %param.16) | copy-start | bytes 52
  11.5 16.8 %copy-start.4 = (bf16[1,16,256]{2,1,0:T(8,128)(2,1)S(1)}, bf16[1,16,256]{2,1,0:T(8,128)(2,1)}, u32[]{:S(2)}) copy-start(bf16[1,16,256]{2,1,0:T(8,128)(2,1)} %param.15) | copy-start | bytes 24580
  26.4 53.7 %copy-start.5 = (s32[1,4]{1,0:T(1,128)S(1)}, s32[1,4]{1,0:T(1,128)}, u32[]{:S(2)}) copy-start(s32[1,4]{1,0:T(1,128)} %param.17) | copy-start | bytes 52
  27.6 407.7 %all-gather.12.cloned.1.call-start = ((), (), s32[]{:S(2)}) async-start(), calls=%async_computation.3 | async-start | bytes 17301504 | tf_op jit(solution)/shard_map/all_gather | solution.py:74
  91.2 82.5 %copy-start.1 = (bf16[384,1024]{1,0:T(8,128)(2,1)S(1)}, bf16[384,1024]{1,0:T(8,128)(2,1)}, u32[]{:S(2)}) copy-start(bf16[384,1024]{1,0:T(8,128)(2,1)} %fusion.9) | copy-start | bytes 2359300
  301.0 150.4 %copy-start.3 = (bf16[384,128]{1,0:T(8,128)(2,1)}, bf16[384,128]{1,0:T(8,128)(2,1)S(1)}, u32[]{:S(2)}) copy-start(bf16[384,128]{1,0:T(8,128)(2,1)S(1)} %fusion.21) | copy-start | bytes 294916
  301.5 147.3 %copy-start.2 = (bf16[384,128]{1,0:T(8,128)(2,1)}, bf16[384,128]{1,0:T(8,128)(2,1)S(1)}, u32[]{:S(2)}) copy-start(bf16[384,128]{1,0:T(8,128)(2,1)S(1)} %get-tuple-element.18) | copy-start | bytes 294916
Sparse Core Ops, SparseCore 0:
  10.6 78.0 all-gather.13
  91.3 76.9 all-gather.9
  170.9 78.0 all-gather.7
  251.3 42.6 all-gather.5
  296.5 138.7 all-gather.11
where the time goes:
time: 463 us; the launch traced here: 461 us
  waiting for transfers between devices  315 us (68%)
  blocking collectives  91.5 us (20%)
  matrix products  30.7 us (7%)
  between operations  14.1 us (3%)
  other arithmetic  6.18 us (1%)
    all_gather x1, waiting for transfers between devices, shards(): lax.all_gather(query_weight, 'req', axis=0, tiled=True)  134 us
    all_gather x1, waiting for transfers between devices, shards(): lax.all_gather(adapter_down, 'req', axis=0, tiled=True)  77.2 us
    all_gather x1, blocking collectives, shards(): lax.all_gather(adapter_up_keyvalue, 'req', axis=0, tiled=True)  51.7 us
    all_gather x1, waiting for transfers between devices, shards(): lax.all_gather(keyvalue_weight, 'req', axis=0, tiled=True)  49.5 us
    all_gather x1, waiting for transfers between devices, shards(): normed = lax.all_gather(normed_part, 'blk', axis=1, tiled=True)  45 us
    psum x1, blocking collectives, shards(): lax.psum(masked, 'blk').reshape(row_number, 3, rank_size)  24.9 us
    dot_general x2, matrix products, add_rows(): return jnp.dot(normed, weight_piece, preferred_element_type=jnp.float32)  18.4 us
    psum x1, blocking collectives, shards(): squares = lax.psum(jnp.sum(values * values, axis=1), 'blk')  14.9 us
  transfers between devices with their start and end apart: 5, of which 5 were waited for; matrix products, arithmetic and copies ran while one was open for 5% of the time, Pallas kernels for 0%

commit v1 on v0

v1 whole, which is shorter than its diff:
```python
import functools
import math

import jax
import jax.numpy as jnp
import numpy as np
from jax import lax
from jax.experimental import pallas as pl
from jax.experimental.pallas import tpu as pltpu
from jax.sharding import PartitionSpec as P

EPSILON = 1e-05
ADAPTER_SCALE = 2.0
ROPE_BASE = 10000.0
HEAD = 128
T = 384
RANK = 16
NZ, NX, NY = 8, 4, 4
WIDTH = 8192
BF, F32 = jnp.bfloat16, jnp.float32

ITEM_UP, ITEM_W0, ITEM_DOWN, ITEM_W1, ITEM_W2, ITEM_W3, ITEM_W4 = range(7)
W_ITEMS = (ITEM_W0, ITEM_W1, ITEM_W2, ITEM_W3, ITEM_W4)


def kernel(
    hid, gain, qw, kvw, down, up_q, up_kv, freq, lens, picks,
    ctx_o, key_o, val_o,
    wg, act, nrm, dg, ug, ssb, avb,
    relay_s, relay_r, fin_s, fin_r, own, hold,
    lrx_s, lrx_r, lrc_s, lrc_r, lry_s, lry_r,
    lhs, bias, cosb, sinb, keys, vals,
    z_send, z_recv, y_send, y_recv, xa_send, xa_recv, xu_send, xu_recv,
    av_send, av_recv, ss_send, ss_recv, d1_send, d1_recv,
    rs_send, rs_recv, lr_send, lr_recv, loc_sem,
):
    b = lax.axis_index("blk")
    r = lax.axis_index("req")
    y, c = lax.div(b, 2), lax.rem(b, 2)
    z, x = lax.div(r, 4), lax.rem(r, 4)
    sgn = 1 - 2 * c

    def dev(zz, xx, yy, cc):
        return {"blk": yy * 2 + cc, "req": zz * 4 + xx}

    def zrel(d):
        return lax.rem(z + d + NZ, NZ)

    def xrel(d):
        return lax.rem(x + d + NX, NX)

    def yrel(d):
        return lax.rem(y + d + NY, NY)

    def remote(src, dst, ssem, rsem, to):
        return pltpu.make_async_remote_copy(
            src_ref=src, dst_ref=dst, send_sem=ssem, recv_sem=rsem,
            device_id=to, device_id_type=pl.DeviceIdType.MESH,
        )

    sent = []

    def go(copy):
        copy.start()
        sent.append(copy)

    def mo(v, m):
        return pl.multiple_of(v, m)

    barrier = pltpu.get_barrier_semaphore()
    peers = [dev(z, xrel(dx), yrel(dy), c) for dx in range(4) for dy in range(4) if dx or dy]
    peers += [dev(z, x, yrel(dy), 1 - c) for dy in range(4)]
    peers += [dev(zrel(1), x, y, c), dev(zrel(-1), x, y, c)]
    for peer in peers:
        pl.semaphore_signal(barrier, inc=1, device_id=peer, device_id_type=pl.DeviceIdType.MESH)

    def krow(q):
        return lax.rem(q, 2) * 4 + lax.div(q, 2)

    own_rows = pl.ds(mo(krow(z) * 256, 256), 256)
    wg[0, own_rows, :] = kvw[...]
    for i in range(4):
        wg[1 + i, own_rows, :] = qw[:, i * 256:(i + 1) * 256]
    up_rows = pl.ds(mo(z * 16, 16), 16)
    ug[up_rows, 0:256] = up_kv[...]
    ug[up_rows, 256:1280] = up_q[...]

    acc = None
    for i in range(8):
        v = hid[:, i * 128:(i + 1) * 128].astype(F32)
        acc = v * v if acc is None else acc + v * v
    ssb[b] = jnp.broadcast_to(jnp.sum(acc.T, axis=0, keepdims=True), (8, T))

    l0, l1, l2 = lens[0, 0], lens[0, 1], lens[0, 2]
    e0, e1, e2 = l0, l0 + l1, l0 + l1 + l2
    row_t = lax.broadcasted_iota(jnp.int32, (8, T), 1)

    def pick(t, v0, v1, v2, v3):
        return jnp.where(t < e0, v0, jnp.where(t < e1, v1, jnp.where(t < e2, v2, v3)))

    avb[0] = pick(row_t, picks[0, 0], picks[0, 1], picks[0, 2], picks[0, 3]).astype(F32)

    pl.semaphore_wait(barrier, len(peers))

    def z_slot(item, h, q):
        if item == ITEM_UP:
            return ug.at[pl.ds(mo(q * 16, 16), 16), :]
        if item == ITEM_DOWN:
            return dg.at[q]
        return wg.at[W_ITEMS.index(item), pl.ds(mo(krow(q) * 256 + h * 128, 128), 128), :]

    def z_copy(item, h, d, step):
        way = sgn if d == 0 else -sgn
        ref = z_slot(item, h, lax.rem(z - way * (step - 1) + NZ, NZ))
        n = ((item * 2 + h) * 2 + d) * 4 + step - 1
        return remote(ref, ref, z_send.at[n], z_recv.at[n], dev(lax.rem(z + way + NZ, NZ), x, y, c))

    def z_wait(item, h, d, step):
        way = sgn if d == 0 else -sgn
        ref = z_slot(item, h, lax.rem(z - way * step + NZ, NZ))
        n = ((item * 2 + h) * 2 + d) * 4 + step - 1
        remote(ref, ref, z_send.at[n], z_recv.at[n], dev(lax.rem(z + way + NZ, NZ), x, y, c)).wait_recv()

    def halves(item):
        return (0,) if item in (ITEM_UP, ITEM_DOWN) else (0, 1)

    def z_start(item):
        for h in halves(item):
            for d in (0, 1):
                go(z_copy(item, h, d, 1))

    def z_step(item, step, hs=None):
        for h in halves(item) if hs is None else hs:
            for d in (0, 1):
                if step == 4 and d == 1:
                    continue
                z_wait(item, h, d, step)
                if step < 3 or (step == 3 and d == 0):
                    go(z_copy(item, h, d, step + 1))

    for p in range(1, 8):
        dy, dc = p // 2, p % 2
        go(remote(ssb.at[b], ssb.at[b], ss_send.at[p], ss_recv.at[p],
                  dev(z, x, yrel(dy), lax.rem(c + dc, 2))))
    z_start(ITEM_UP)
    for d in range(4):
        def copy(d=d):
            return remote(
                down.at[:, pl.ds(mo(xrel(d) * 256, 256), 256)],
                dg.at[z, :, pl.ds(mo(y * 256, 256), 256)],
                d1_send.at[d], d1_recv.at[y], dev(z, xrel(d), x, c))
        if d:
            go(copy())
        else:
            @pl.when(y == x)
            def _():
                pltpu.make_async_copy(
                    down.at[:, pl.ds(mo(x * 256, 256), 256)],
                    dg.at[z, :, pl.ds(mo(y * 256, 256), 256)], d1_recv.at[y]).start()

            @pl.when(y != x)
            def _():
                copy().start()
    z_start(ITEM_W0)
    for d in range(1, 4):
        go(remote(avb.at[0], avb.at[(4 - d) % 4], av_send.at[d], av_recv.at[d], dev(z, xrel(d), y, c)))

    col_t = lax.broadcasted_iota(jnp.int32, (T, HEAD), 0)
    position = col_t - pick(col_t, 0, e0, e1, e2)
    angles = position.astype(F32) * freq[0:1, :]
    cosb[...] = jnp.cos(angles)
    lane = lax.broadcasted_iota(jnp.int32, (T, HEAD), 1)
    sines = jnp.sin(angles)
    sinb[...] = jnp.where(lane < HEAD // 2, -sines, sines)

    z_step(ITEM_UP, 1)

    for p in range(1, 8):
        dy, dc = p // 2, p % 2
        q = yrel(-dy) * 2 + lax.rem(c + dc, 2)
        remote(ssb.at[q], ssb.at[q], ss_send.at[p], ss_recv.at[p],
               dev(z, x, yrel(dy), lax.rem(c + dc, 2))).wait_recv()
    total = ssb[0]
    for i in range(1, 8):
        total = total + ssb[i]
    factor = lax.rsqrt(total / WIDTH + EPSILON)
    factor = jnp.broadcast_to(factor[0:1, :], (HEAD, T)).T
    gains = gain[pl.ds(mo(b * 8, 8), 8), :]
    for i in range(8):
        v = hid[:, i * 128:(i + 1) * 128].astype(F32)
        nrm[:, i * 128:(i + 1) * 128] = (v * factor * gains[i:i + 1, :]).astype(BF)

    own_cols = pl.ds(mo((c * 4 + y) * 256, 256), 256)
    quarter = pl.ds(mo(x * 256, 256), 256)

    def xa(d):
        return remote(
            nrm.at[:, pl.ds(mo(xrel(d) * 256, 256), 256)], act.at[(4 - d) % 4, :, own_cols],
            xa_send.at[d], xa_recv.at[d], dev(z, xrel(d), y, c))

    def y_cols(yy):
        return pl.ds(mo((c * 4 + yy) * 256, 256), 256)

    def y_copy(k, n):
        if n < 2:
            src = nrm.at[:, quarter] if k == 0 else act.at[k, :, own_cols]
            dst = act.at[k, :, own_cols]
            to = dev(z, x, yrel(1 - 2 * n), c)
        elif n == 2:
            src = dst = act.at[k, 0:192, y_cols(yrel(-1))]
            to = dev(z, x, yrel(1), c)
        elif n == 3:
            src = dst = act.at[k, 192:384, y_cols(yrel(1))]
            to = dev(z, x, yrel(-1), c)
        else:
            src = dst = act.at[k, :, pl.ds(mo(c * 1024, 1024), 1024)]
            to = dev(z, x, y, 1 - c)
        return remote(src, dst, y_send.at[k * 5 + n], y_recv.at[k * 5 + n], to)

    def y_wait(k, n):
        if n < 2:
            dst = act.at[k, :, y_cols(yrel(2 * n - 1))]
        elif n == 2:
            dst = act.at[k, 0:192, y_cols(yrel(2))]
        elif n == 3:
            dst = act.at[k, 192:384, y_cols(yrel(2))]
        else:
            dst = act.at[k, :, pl.ds(mo((1 - c) * 1024, 1024), 1024)]
        remote(dst, dst, y_send.at[k * 5 + n], y_recv.at[k * 5 + n], dev(z, x, y, 1 - c)).wait_recv()

    own_copy = pltpu.make_async_copy(nrm.at[:, quarter], act.at[0, :, own_cols], loc_sem.at[0])

    def y_begin(k):
        if k:
            xa_k = remote(act.at[k, :, own_cols], act.at[k, :, own_cols], xa_send.at[4 - k], xa_recv.at[4 - k],
                          dev(z, xrel(1), y, c))
            xa_k.wait_recv()
        for n in (0, 1):
            go(y_copy(k, n))

    def y_middle(k):
        for n in (0, 1):
            y_wait(k, n)
            go(y_copy(k, n + 2))

    def y_end(k):
        for n in (2, 3):
            y_wait(k, n)
        if k == 0:
            own_copy.wait()
        go(y_copy(k, 4))

    def y_done(k):
        y_wait(k, 4)

    y_begin(0)
    for d in (2, 1, 3):
        go(xa(d))
    own_copy.start()

    def xu(d):
        return remote(ug.at[0:128, :], ug.at[pl.ds(((4 - d) % 4) * 128, 128), :],
                      xu_send.at[d], xu_recv.at[d], dev(z, xrel(d), y, c))

    def lrx(k):
        return remote(lrx_s.at[k], lrx_r.at[k], lr_send.at[k], lr_recv.at[k], dev(z, xrel(k), y, c))

    def low_partial(k):
        part = lax.dot_general(
            dg[...].reshape(NZ * 48, 1024), act[k, :, pl.ds(mo(c * 1024, 1024), 1024)],
            (((1,), (1,)), ((), ())), preferred_element_type=F32)
        ids = avb[k, 0:1, :]
        out = None
        for q in range(NZ):
            hit = ids == (4 * q + y).astype(F32)
            term = jnp.where(hit, part[q * 48:(q + 1) * 48, :], 0.0)
            out = term if out is None else out + term
        lrx_s[k] = out
        if k:
            go(lrx(k))

    def low_core():
        total = lrx_s[0]
        for k in range(1, 4):
            lrx(k).wait_recv()
            total = total + lrx_r[k]
        lrc_s[...] = total
        go(remote(lrc_s, lrc_r, lr_send.at[4], lr_recv.at[4], dev(z, x, y, 1 - c)))

    def lry(d):
        return remote(lry_s, lry_r.at[d], lr_send.at[4 + d], lr_recv.at[4 + d], dev(z, x, yrel(d), c))

    def low_y():
        remote(lrc_s, lrc_r, lr_send.at[4], lr_recv.at[4], dev(z, x, y, 1 - c)).wait_recv()
        lry_s[...] = lrc_s[...] + lrc_r[...]
        for d in range(1, 4):
            go(lry(d))

    def low_end():
        total = lry_s[...]
        for d in range(1, 4):
            lry(d).wait_recv()
            total = total + lry_r[d]
        low = total.astype(BF)
        row = lax.broadcasted_iota(jnp.int32, (512, RANK), 0)
        rank = lax.broadcasted_iota(jnp.int32, (512, RANK), 1)
        repeat = ((row & 15) == rank).astype(BF)
        row = lax.broadcasted_iota(jnp.int32, (512, T), 0)
        adapter = 4 * ((row & 127) >> 4) + ((x + (row >> 7)) & 3)
        hit = adapter.astype(F32) == avb[0, 0:1, :]
        for j in range(3):
            spread = jnp.dot(repeat, low[j * RANK:(j + 1) * RANK, :], preferred_element_type=F32)
            lhs[j] = jnp.where(hit, spread, 0.0).T.astype(BF)

    def make_bias():
        tc = lax.broadcasted_iota(jnp.int32, (T, T), 0)
        tr = lax.broadcasted_iota(jnp.int32, (T, T), 1)
        allowed = (pick(tc, 0, 1, 2, 3) == pick(tr, 0, 1, 2, 3)) & (tr <= tc)
        bias[...] = jnp.where(allowed, 0.0, -1e30)

    def part(k, j):
        return jnp.dot(act[k], wg[j], preferred_element_type=F32)

    def relay(j, d):
        return remote(relay_s.at[j, d], relay_r.at[j, d], rs_send.at[j * 4 + d], rs_recv.at[j * 4 + d],
                      dev(z, xrel(1 - 2 * d), y, c))

    def final(j, d):
        return remote(fin_s.at[j, d], fin_r.at[j, d], rs_send.at[j * 4 + 2 + d], rs_recv.at[j * 4 + 2 + d],
                      dev(z, xrel(1 - 2 * d), y, c))

    def rs_far(j):
        p = part(2, j).astype(BF)
        for d in (0, 1):
            relay_s[j, d] = p[d * 192:(d + 1) * 192]
            go(relay(j, d))

    def rs_hold(j, d):
        hold[d] = part(1 if d == 0 else 3, j)

    def rs_near(j, d):
        relay(j, d).wait_recv()
        lo = d * 192
        fin_s[j, d, lo:lo + 192] = (hold[d, lo:lo + 192] + relay_r[j, d].astype(F32)).astype(BF)
        fin_s[j, d, 192 - lo:384 - lo] = hold[d, 192 - lo:384 - lo].astype(BF)
        go(final(j, d))

    def rs_own(j):
        own[...] = part(0, j)

    def rotate(v):
        return v * cosb[...] + pltpu.roll(v, HEAD // 2, axis=1) * sinb[...]

    def chunk_end(j):
        base = own[...]
        for d in (0, 1):
            final(j, d).wait_recv()
            base = base + fin_r[j, d].astype(F32)
        ups = ug[:, j * 256:(j + 1) * 256]
        if j == 0:
            k = base[:, 0:128] + ADAPTER_SCALE * jnp.dot(lhs[1], ups[:, 0:128], preferred_element_type=F32)
            v = base[:, 128:256] + ADAPTER_SCALE * jnp.dot(lhs[2], ups[:, 128:256], preferred_element_type=F32)
            k, v = rotate(k).astype(BF), v.astype(BF)
            keys[...] = k
            vals[...] = v
            key_o[...] = k
            val_o[...] = v
            return
        base = base + ADAPTER_SCALE * jnp.dot(lhs[0], ups, preferred_element_type=F32)
        for i in range(2):
            q = rotate(base[:, i * 128:(i + 1) * 128]).astype(BF)
            head = ((j - 1) * 2 + i) * 128
            for n in range(3):
                rows, wide = slice(n * 128, (n + 1) * 128), (n + 1) * 128
                s = lax.dot_general(q[rows], keys[0:wide, :], (((1,), (1,)), ((), ())),
                                    preferred_element_type=F32)
                s = s * (1.0 / math.sqrt(HEAD)) + bias[rows, 0:wide]
                e = jnp.exp(s - jnp.max(s, axis=1, keepdims=True))
                a = (e / jnp.sum(e, axis=1, keepdims=True)).astype(BF)
                o = jnp.dot(a, vals[0:wide, :], preferred_element_type=F32)
                ctx_o[rows, head:head + 128] = o.astype(BF)

    z_step(ITEM_W0, 1)
    z_step(ITEM_UP, 2)
    z_step(ITEM_W0, 2)
    for q in range(4):
        ref = dg.at[z, :, q * 256:(q + 1) * 256]
        remote(ref, ref, d1_send.at[0], d1_recv.at[q], dev(z, xrel(1), y, c)).wait_recv()
    z_start(ITEM_DOWN)
    y_middle(0)
    z_step(ITEM_UP, 3)
    z_step(ITEM_W0, 3)
    z_start(ITEM_W1)
    y_end(0)
    y_begin(2)
    z_step(ITEM_UP, 4)
    for d in (1, 3, 2):
        go(xu(d))
    y_begin(1)
    y_begin(3)
    z_step(ITEM_DOWN, 1)
    z_step(ITEM_W0, 4)
    make_bias()
    z_step(ITEM_W1, 1)
    y_done(0)
    z_step(ITEM_DOWN, 2)
    y_middle(2)
    z_step(ITEM_W1, 2)
    y_end(2)
    y_middle(1)
    z_step(ITEM_DOWN, 3)
    z_step(ITEM_W1, 3, (0,))
    z_step(ITEM_W1, 3, (1,))
    z_start(ITEM_W2)
    y_end(1)
    z_step(ITEM_DOWN, 4)
    y_middle(3)
    z_step(ITEM_W1, 4)
    y_end(3)
    y_done(2)
    for d in (1, 2, 3):
        remote(avb.at[0], avb.at[(4 - d) % 4], av_send.at[d], av_recv.at[d], dev(z, xrel(d), y, c)).wait_recv()
    rs_far(0)
    z_step(ITEM_W2, 1, (0,))
    low_partial(2)
    z_step(ITEM_W2, 1, (1,))
    y_done(1)
    low_partial(1)
    rs_hold(0, 0)
    z_step(ITEM_W2, 2, (0,))
    rs_near(0, 0)
    y_done(3)
    low_partial(3)
    rs_hold(0, 1)
    z_step(ITEM_W2, 2, (1,))
    rs_near(0, 1)
    rs_far(1)
    low_partial(0)
    z_step(ITEM_W2, 3, (0,))
    rs_own(0)
    low_core()
    z_step(ITEM_W2, 3, (1,))
    z_start(ITEM_W3)
    rs_hold(1, 0)
    rs_near(1, 0)
    low_y()
    z_step(ITEM_W2, 4, (0,))
    rs_hold(1, 1)
    rs_near(1, 1)
    z_step(ITEM_W2, 4, (1,))
    rs_far(2)
    z_step(ITEM_W3, 1, (0,))
    low_end()
    z_step(ITEM_W3, 1, (1,))
    for d in (1, 2, 3):
        xu(d).wait_recv()
    chunk_end(0)
    z_step(ITEM_W3, 2, (0,))
    rs_own(1)
    rs_hold(2, 0)
    z_step(ITEM_W3, 2, (1,))
    rs_near(2, 0)
    rs_hold(2, 1)
    rs_near(2, 1)
    z_step(ITEM_W3, 3, (0,))
    chunk_end(1)
    z_step(ITEM_W3, 3, (1,))
    z_start(ITEM_W4)
    rs_own(2)
    z_step(ITEM_W3, 4, (0,))
    chunk_end(2)
    z_step(ITEM_W3, 4, (1,))
    rs_far(3)
    z_step(ITEM_W4, 1, (0,))
    rs_hold(3, 0)
    z_step(ITEM_W4, 1, (1,))
    rs_near(3, 0)
    rs_hold(3, 1)
    rs_near(3, 1)
    z_step(ITEM_W4, 2, (0,))
    rs_own(3)
    z_step(ITEM_W4, 2, (1,))
    z_step(ITEM_W4, 3, (0,))
    z_step(ITEM_W4, 3, (1,))
    chunk_end(3)
    z_step(ITEM_W4, 4, (0,))
    z_step(ITEM_W4, 4, (1,))
    rs_far(4)
    rs_hold(4, 0)
    rs_near(4, 0)
    rs_hold(4, 1)
    rs_near(4, 1)
    rs_own(4)
    chunk_end(4)

    for copy in sent:
        copy.wait_send()

    @pl.when(y != x)
    def _():
        remote(down.at[:, pl.ds(mo(x * 256, 256), 256)], dg.at[z, :, pl.ds(mo(y * 256, 256), 256)],
               d1_send.at[0], d1_recv.at[y], dev(z, x, x, c)).wait_send()


def shards(hidden, gain, qw, kvw, down, up_q, up_kv, lens, picks):
    half = np.arange(HEAD // 2, dtype=np.float32) * np.float32(2.0) / np.float32(HEAD)
    one = np.power(np.float32(ROPE_BASE), -half).astype(np.float32)
    freq = jnp.asarray(np.tile(np.concatenate([one, one])[None, :], (8, 1)))
    vmem, smem = pl.BlockSpec(memory_space=pltpu.VMEM), pl.BlockSpec(memory_space=pltpu.SMEM)
    dma = pltpu.SemaphoreType.DMA
    scratch = [
        pltpu.VMEM((5, 2048, 256), BF),
        pltpu.VMEM((4, T, 2048), BF),
        pltpu.VMEM((T, 1024), BF),
        pltpu.VMEM((8, 48, 1024), BF),
        pltpu.VMEM((512, 1280), BF),
        pltpu.VMEM((8, 8, T), F32),
        pltpu.VMEM((4, 8, T), F32),
        pltpu.VMEM((5, 2, 192, 256), BF),
        pltpu.VMEM((5, 2, 192, 256), BF),
        pltpu.VMEM((5, 2, T, 256), BF),
        pltpu.VMEM((5, 2, T, 256), BF),
        pltpu.VMEM((T, 256), F32),
        pltpu.VMEM((2, T, 256), F32),
        pltpu.VMEM((4, 48, T), F32),
        pltpu.VMEM((4, 48, T), F32),
        pltpu.VMEM((48, T), F32),
        pltpu.VMEM((48, T), F32),
        pltpu.VMEM((48, T), F32),
        pltpu.VMEM((4, 48, T), F32),
        pltpu.VMEM((3, T, 512), BF),
        pltpu.VMEM((T, T), F32),
        pltpu.VMEM((T, HEAD), F32),
        pltpu.VMEM((T, HEAD), F32),
        pltpu.VMEM((T, HEAD), BF),
        pltpu.VMEM((T, HEAD), BF),
        dma((112,)), dma((112,)),
        dma((20,)), dma((20,)),
        dma((4,)), dma((4,)),
        dma((4,)), dma((4,)),
        dma((4,)), dma((4,)),
        dma((8,)), dma((8,)),
        dma((4,)), dma((4,)),
        dma((20,)), dma((20,)),
        dma((8,)), dma((8,)),
        dma((1,)),
    ]
    return pl.pallas_call(
        kernel,
        out_shape=(
            jax.ShapeDtypeStruct((T, 1024), BF),
            jax.ShapeDtypeStruct((T, HEAD), BF),
            jax.ShapeDtypeStruct((T, HEAD), BF),
        ),
        in_specs=[vmem] * 8 + [smem] * 2,
        out_specs=(vmem, vmem, vmem),
        scratch_shapes=scratch,
        compiler_params=pltpu.CompilerParams(
            collective_id=0, has_side_effects=True, vmem_limit_bytes=56 * 1024 * 1024
        ),
        cost_estimate=pl.CostEstimate(flops=10_000_000_000, bytes_accessed=4_000_000, transcendentals=1_500_000),
    )(
        hidden, gain.reshape(64, 128), qw, kvw, down.reshape(48, 1024),
        up_q.reshape(16, 1024), up_kv.reshape(16, 256), freq, lens, picks,
    )


def solution(mesh):
    in_specs = (
        P("req", "blk"), P(), P("req", "blk"), P("req", "blk"), P("req", None, None, "blk"),
        P("req", None, "blk"), P("req", None, "blk"), P("req", None), P("req", None),
    )
    out_specs = (P("req", "blk"), P("req", "blk"), P("req", "blk"))
    return jax.shard_map(shards, mesh=mesh, in_specs=in_specs, out_specs=out_specs, check_vma=False)
```

time: 463 us -> 120 us (0.26)
  waiting for transfers between devices: 315 us -> 0 us
  Pallas kernels: 0 us -> 116 us
  blocking collectives: 91.5 us -> 0 us
  matrix products: 30.7 us -> 0 us
  between operations: 14.1 us -> 0.65 us
  other arithmetic: 6.18 us -> 0 us
    all_gather x5 -> x0, waiting for transfers between devices: 313 us -> none  [the longest x1 134 us: shards(): lax.all_gather(query_weight, 'req', axis=0, tiled=True)]
    pallas_call x0 -> x1, Pallas kernels: none -> 116 us  [shards(): pl.pallas_call(kernel, out_shape=(jax.ShapeDtypeStruct((T, 1024), BF), ja...]
    all_gather x1 -> x0, blocking collectives: 51.7 us -> none  [shards(): lax.all_gather(adapter_up_keyvalue, 'req', axis=0, tiled=True)]
    psum x2 -> x0, blocking collectives: 39.8 us -> none  [the longest x1 24.9 us: shards(): lax.psum(masked, 'blk').reshape(row_number, 3, rank_size)]
    dot_general x11 -> x0, matrix products: 30.7 us -> none  [the longest x2 18.4 us: add_rows(): return jnp.dot(normed, weight_piece, preferred_element_type=jnp.float32)]
  transfers between devices with their start and end apart: 5 -> 0, of which waited for: 5 -> 0; matrix products, arithmetic and copies ran while one was open for 5% -> 0% of each run, Pallas kernels for 0% -> 0%
where the time goes in v1:
time: 120 us
  Pallas kernels  116 us (97%)
  local copies, waits for them, and re-layouts  3.67 us (3%)
    pallas_call x1, Pallas kernels, shards(): pl.pallas_call(kernel, out_shape=(jax.ShapeDtypeStruct((T, 1024), BF), ja...  116 us
    unnamed x7, local copies, waits for them, and re-layouts  3.67 us

profile of v1, /device:TPU:6, one launch (start us, length us, event | category | flops | bytes accessed | tf_op | source)
XLA Modules:
  0.0 120.0 jit_solution(16965755874211979645)
XLA Ops:
  0.6 115.6 %shard_map.121 = (bf16[384,1024]{1,0:T(8,128)(2,1)}, bf16[384,128]{1,0:T(8,128)(2,1)}, bf16[384,128]{1,0:T(8,128)(2,1)}) custom-call(bf16[384,1024]{1,0:T(8,128)(2,1)} %hid.1, f32[64,128]{1,0:T(8,128)} %bitcast.5, bf16[256,1024]{1,0:T(8,128)(2,1)} %qw.1, bf16[256,256]{1,0:T(8,128)(2,1)} %kvw.1, bf16[48,1024]{1,0:T(8,128)(2,1)} %bitcast.4, ...), custom_call_target="tpu_custom_call" | custom-call | flops 10000000000 | bytes 4000000 | tf_op jit(solution)/shard_map/pallas_call | solution.py:548
  116.3 0.0 copy-start.1
  116.3 2.1 %copy.16 = bf16[384,1024]{1,0:T(8,128)(2,1)} copy(bf16[384,1024]{1,0:T(8,128)(2,1)} %get-tuple-element.6) | data formatting | bytes 1572864
  118.4 0.0 copy-done.1
  118.4 0.0 copy-start
  118.4 0.6 copy.17
  119.0 0.3 copy-done
  119.3 0.6 copy.18
Async XLA Ops:
  116.3 2.1 %copy-start.1 = (bf16[384,128]{1,0:T(8,128)(2,1)S(1)}, bf16[384,128]{1,0:T(8,128)(2,1)}, u32[]{:S(2)}) copy-start(bf16[384,128]{1,0:T(8,128)(2,1)} %get-tuple-element.7) | copy-start | bytes 294916
  118.4 0.9 copy-start

commit v2 on v1

v2 whole, which is shorter than its diff:
```python
import functools
import math

import jax
import jax.numpy as jnp
import numpy as np
from jax import lax
from jax.experimental import pallas as pl
from jax.experimental.pallas import tpu as pltpu
from jax.sharding import PartitionSpec as P

EPSILON = 1e-05
ADAPTER_SCALE = 2.0
ROPE_BASE = 10000.0
HEAD = 128
T = 384
RANK = 16
NZ, NX, NY = 8, 4, 4
WIDTH = 8192
BF, F32 = jnp.bfloat16, jnp.float32

WIDTHS = (256, 256, 128, 128, 128, 128, 128, 128)
STARTS = tuple(sum(WIDTHS[:j]) for j in range(len(WIDTHS)))
CHUNKS = len(WIDTHS)
ITEMS = ("U", "D") + tuple(range(CHUNKS))

ORDER = (
    ("begin",), ("yb", 0), ("xs",), ("zs", 0), ("zs", 1), ("tables",), ("bias",), ("fac",), ("zw", 0, 0, 1),
    ("ym", 0, 0), ("ym", 0, 1), ("zw", 0, 1, 1), ("zs", "U"), ("ys", 0, 0), ("ys", 0, 1), ("zw", 1, 0, 1), ("yb", 2),
    ("zw", 1, 1, 1), ("sw",), ("ye", 0), ("zw", 0, 0, 2), ("yd", 0), ("yb", 1), ("zw", 0, 1, 2), ("zw", "U", 0, 1),
    ("ym", 2, 0), ("ym", 2, 1), ("zw", "U", 1, 1), ("yb", 3), ("zw", 1, 0, 2), ("ys", 2, 0), ("ys", 2, 1),
    ("zw", 1, 1, 2), ("ym", 1, 0), ("ym", 1, 1), ("zw", 0, 0, 3), ("zw", 0, 1, 3), ("zw", "U", 0, 2), ("ys", 1, 0),
    ("ys", 1, 1), ("zw", "U", 1, 2), ("zs", "D"), ("zw", 1, 0, 3), ("ye", 2), ("zw", 1, 1, 3), ("zs", 2), ("yd", 2),
    ("ym", 3, 0), ("ym", 3, 1), ("zw", 0, 0, 4), ("far", 0), ("zw", "U", 0, 3), ("own", 0), ("zw", "U", 1, 3),
    ("zs", 3), ("ys", 3, 0), ("ys", 3, 1), ("zw", "D", 0, 1), ("zw", "D", 1, 1), ("zs", 5), ("ye", 1),
    ("zw", 1, 0, 4), ("far", 1), ("own", 1), ("zw", 2, 0, 1), ("yd", 1), ("zw", 2, 1, 1), ("ye", 3), ("near", 0, 0),
    ("zw", "U", 0, 4), ("up", 1), ("up", 2), ("zw", 3, 0, 1), ("up", 3), ("yd", 3), ("zw", 3, 1, 1), ("near", 0, 1),
    ("up", 0), ("zw", "D", 0, 2), ("near", 1, 0), ("near", 1, 1), ("zw", "D", 1, 2), ("zw", 5, 0, 1), ("zw", 5, 1, 1),
    ("zw", 2, 0, 2), ("zw", 2, 1, 2), ("zw", 3, 0, 2), ("zw", 3, 1, 2), ("zw", "D", 0, 3), ("zw", "D", 1, 3),
    ("zw", 5, 0, 2), ("zw", 5, 1, 2), ("zs", 6), ("zw", 2, 0, 3), ("zw", 2, 1, 3), ("zw", 3, 0, 3), ("zw", 3, 1, 3),
    ("uw",), ("zw", "D", 0, 4), ("zs", 4), ("lp", 0), ("lp", 1), ("lp", 2), ("zw", 5, 0, 3), ("lp", 3),
    ("zw", 5, 1, 3), ("zw", 6, 0, 1), ("zw", 6, 1, 1), ("zs", 7), ("zw", 2, 0, 4), ("far", 2), ("own", 2),
    ("zw", 3, 0, 4), ("far", 3), ("own", 3), ("zw", 4, 0, 1), ("zw", 4, 1, 1), ("zw", 5, 0, 4), ("far", 5),
    ("own", 5), ("lc",), ("zw", 6, 0, 2), ("near", 2, 0), ("zw", 6, 1, 2), ("near", 2, 1), ("ly",), ("zw", 7, 0, 1),
    ("near", 3, 0), ("near", 3, 1), ("zw", 7, 1, 1), ("near", 5, 0), ("zw", 4, 0, 2), ("near", 5, 1), ("zw", 4, 1, 2),
    ("zw", 6, 0, 3), ("zw", 6, 1, 3), ("zw", 7, 0, 2), ("zw", 7, 1, 2), ("zw", 4, 0, 3), ("le",), ("zw", 4, 1, 3),
    ("end", 0, 0), ("zw", 6, 0, 4), ("far", 6), ("zw", 7, 0, 3), ("own", 6), ("end", 1, 0), ("zw", 4, 0, 4),
    ("zw", 7, 1, 3), ("far", 4), ("own", 4), ("end", 1, 1), ("zw", 7, 0, 4), ("near", 6, 0), ("near", 6, 1),
    ("far", 7), ("own", 7), ("end", 2, 0), ("near", 4, 0), ("near", 4, 1), ("end", 3, 0), ("end", 5, 0),
    ("near", 7, 0), ("near", 7, 1), ("end", 6, 0), ("end", 4, 0), ("end", 7, 0),
)


def kernel(
    hid, gain, qw, kvw, down, up_q, up_kv, freq, lens, picks,
    ctx_o, key_o, val_o,
    wg, act, raw, dg, ug, ssb, avb, gains,
    relay_s, relay_r, fin_s, fin_r, own,
    lrx_s, lrx_r, lrc_s, lrc_r, lry_s, lry_r,
    lhs, bias, cosb, sinb, keys, vals, xus, xur, usel,
    z_send, z_recv, y_send, y_recv, xa_send, xa_recv, xu_send, xu_recv,
    av_send, av_recv, ss_send, ss_recv, d1_send, d1_recv,
    rs_send, rs_recv, lr_send, lr_recv, loc_sem,
):
    b = lax.axis_index("blk")
    r = lax.axis_index("req")
    y, c = lax.div(b, 2), lax.rem(b, 2)
    z, x = lax.div(r, 4), lax.rem(r, 4)
    sgn = 1 - 2 * c

    def dev(zz, xx, yy, cc):
        return {"blk": yy * 2 + cc, "req": zz * 4 + xx}

    def zrel(d):
        return lax.rem(z + d + NZ, NZ)

    def xrel(d):
        return lax.rem(x + d + NX, NX)

    def yrel(d):
        return lax.rem(y + d + NY, NY)

    def remote(src, dst, ssem, rsem, to):
        return pltpu.make_async_remote_copy(
            src_ref=src, dst_ref=dst, send_sem=ssem, recv_sem=rsem,
            device_id=to, device_id_type=pl.DeviceIdType.MESH,
        )

    sent = []

    def go(copy):
        copy.start()
        sent.append(copy)

    def mo(v, m):
        return pl.multiple_of(v, m)

    barrier = pltpu.get_barrier_semaphore()
    peers = [dev(z, xrel(dx), yrel(dy), c) for dx in range(4) for dy in range(4) if dx or dy]
    peers += [dev(z, x, yrel(dy), 1 - c) for dy in range(4)]
    peers += [dev(zrel(1), x, y, c), dev(zrel(-1), x, y, c)]
    for peer in peers:
        pl.semaphore_signal(barrier, inc=1, device_id=peer, device_id_type=pl.DeviceIdType.MESH)

    def krow(q):
        return lax.rem(q, 2) * 4 + lax.div(q, 2)

    own_rows = pl.ds(mo(krow(z) * 256, 256), 256)
    wg[0][own_rows, :] = kvw[...]
    for j in range(1, CHUNKS):
        wg[j][own_rows, :] = qw[:, STARTS[j] - 256:STARTS[j] - 256 + WIDTHS[j]]
    up_rows = pl.ds(mo(z * 16, 16), 16)
    ug[up_rows, 0:256] = up_kv[...]
    ug[up_rows, 256:1280] = up_q[...]

    acc = None
    for i in range(8):
        v = hid[:, i * 128:(i + 1) * 128].astype(F32)
        acc = v * v if acc is None else acc + v * v
    ssb[b] = jnp.broadcast_to(jnp.sum(acc.T, axis=0, keepdims=True), (8, T))

    l0, l1, l2 = lens[0, 0], lens[0, 1], lens[0, 2]
    e0, e1, e2 = l0, l0 + l1, l0 + l1 + l2
    row_t = lax.broadcasted_iota(jnp.int32, (8, T), 1)

    def pick(t, v0, v1, v2, v3):
        return jnp.where(t < e0, v0, jnp.where(t < e1, v1, jnp.where(t < e2, v2, v3)))

    ids = pick(row_t, picks[0, 0], picks[0, 1], picks[0, 2], picks[0, 3])
    slot = row_t >> 4
    by_prompt = jnp.where(slot == 0, picks[0, 0], jnp.where(slot == 1, picks[0, 1], jnp.where(
        slot == 2, picks[0, 2], jnp.where(slot == 3, picks[0, 3], -1))))
    side_row = lax.broadcasted_iota(jnp.int32, (8, T), 0)
    avb[0, 8:16, :] = jnp.where(side_row == 0, ids, by_prompt).astype(F32)

    pl.semaphore_wait(barrier, len(peers))

    def z_slot(item, q):
        if item == "U":
            return ug.at[pl.ds(mo(q * 16, 16), 16), :]
        if item == "D":
            return dg.at[q]
        return wg[item].at[pl.ds(mo(krow(q) * 256, 256), 256), :]

    def z_copy(item, d, step):
        way = sgn if d == 0 else -sgn
        ref = z_slot(item, lax.rem(z - way * (step - 1) + NZ, NZ))
        n = (ITEMS.index(item) * 2 + d) * 4 + step - 1
        return remote(ref, ref, z_send.at[n], z_recv.at[n], dev(lax.rem(z + way + NZ, NZ), x, y, c))

    def z_start(item):
        if item == "D":
            for q in range(4):
                ref = dg.at[z, :, q * 256:(q + 1) * 256]
                remote(ref, ref, d1_send.at[0], d1_recv.at[q], dev(z, xrel(1), y, c)).wait_recv()
        for d in (0, 1):
            go(z_copy(item, d, 1))

    def z_step(item, d, step):
        way = sgn if d == 0 else -sgn
        ref = z_slot(item, lax.rem(z - way * step + NZ, NZ))
        n = (ITEMS.index(item) * 2 + d) * 4 + step - 1
        remote(ref, ref, z_send.at[n], z_recv.at[n], dev(lax.rem(z + way + NZ, NZ), x, y, c)).wait_recv()
        if step < 3 or (step == 3 and d == 0):
            go(z_copy(item, d, step + 1))

    def begin():
        for p in range(1, 8):
            dy, dc = p // 2, p % 2
            go(remote(ssb.at[b], ssb.at[b], ss_send.at[p], ss_recv.at[p],
                      dev(z, x, yrel(dy), lax.rem(c + dc, 2))))
        for d in range(4):
            def copy(d=d):
                return remote(
                    down.at[:, pl.ds(mo(xrel(d) * 256, 256), 256)],
                    dg.at[z, :, pl.ds(mo(y * 256, 256), 256)],
                    d1_send.at[d], d1_recv.at[y], dev(z, xrel(d), x, c))
            if d:
                go(copy())
            else:
                @pl.when(y == x)
                def _():
                    pltpu.make_async_copy(
                        down.at[:, pl.ds(mo(x * 256, 256), 256)],
                        dg.at[z, :, pl.ds(mo(y * 256, 256), 256)], d1_recv.at[y]).start()

                @pl.when(y != x)
                def _():
                    copy().start()

    def tables():
        col_t = lax.broadcasted_iota(jnp.int32, (T, HEAD), 0)
        position = col_t - pick(col_t, 0, e0, e1, e2)
        angles = position.astype(F32) * freq[0:1, :]
        cosb[...] = jnp.cos(angles)
        lane = lax.broadcasted_iota(jnp.int32, (T, HEAD), 1)
        sines = jnp.sin(angles)
        sinb[...] = jnp.where(lane < HEAD // 2, -sines, sines)

    def side(d):
        return remote(avb.at[0], avb.at[(4 - d) % 4], av_send.at[d], av_recv.at[d], dev(z, xrel(d), y, c))

    def factors():
        for p in range(1, 8):
            dy, dc = p // 2, p % 2
            q = yrel(-dy) * 2 + lax.rem(c + dc, 2)
            remote(ssb.at[q], ssb.at[q], ss_send.at[p], ss_recv.at[p],
                   dev(z, x, yrel(dy), lax.rem(c + dc, 2))).wait_recv()
        total = ssb[0]
        for i in range(1, 8):
            total = total + ssb[i]
        avb[0, 0:8, :] = lax.rsqrt(total / WIDTH + EPSILON)
        for d in (1, 2, 3):
            go(side(d))
        row = lax.broadcasted_iota(jnp.int32, (8, 128), 0)
        for n in range(16):
            slot, h = n // 2, n % 2
            q = (slot % 4) * 2 + slot // 4
            mine = jnp.where(row == x * 2 + h, gain[q * 8:(q + 1) * 8, :], 0.0)
            gains[0:1, n * 128:(n + 1) * 128] = jnp.sum(mine, axis=0, keepdims=True)

    def sides():
        for d in (1, 2, 3):
            side(d).wait_recv()

    def norm(k):
        if k == 0:
            own_copy.wait()
        factor = jnp.broadcast_to(avb[k, 0:1, :], (HEAD, T)).T
        for n in range(16):
            cols = slice(n * 128, (n + 1) * 128)
            act[k, :, cols] = (raw[k, :, cols].astype(F32) * factor * gains[0:1, cols]).astype(BF)

    own_cols = pl.ds(mo((c * 4 + y) * 256, 256), 256)
    quarter = pl.ds(mo(x * 256, 256), 256)

    def xa(d):
        return remote(
            hid.at[:, pl.ds(mo(xrel(d) * 256, 256), 256)], raw.at[(4 - d) % 4, :, own_cols],
            xa_send.at[d], xa_recv.at[d], dev(z, xrel(d), y, c))

    def y_cols(cc, yy):
        return pl.ds(mo((cc * 4 + yy) * 256, 256), 256)

    LOW, HIGH = slice(0, 192), slice(192, 384)

    def y_copy(k, n):
        rows = (LOW, HIGH, HIGH, LOW, LOW, HIGH, slice(0, T), slice(0, T), slice(0, T), slice(0, T))[n]
        from_y = (0, 0, 0, 0, -1, 1, 0, -1, 1, 2)[n]
        to = dev(z, x, yrel((1, 1, -1, -1, 1, -1, 0, 0, 0, 0)[n]), c if n < 6 else 1 - c)
        dst = raw.at[k, rows, y_cols(c, yrel(from_y))]
        src = hid.at[rows, quarter] if k == 0 and from_y == 0 else dst
        return remote(src, dst, y_send.at[k * 10 + n], y_recv.at[k * 10 + n], to)

    def y_wait(k, n):
        rows = (LOW, HIGH, HIGH, LOW, LOW, HIGH, slice(0, T), slice(0, T), slice(0, T), slice(0, T))[n]
        from_y = (-1, -1, 1, 1, 2, 2, 0, -1, 1, 2)[n]
        dst = raw.at[k, rows, y_cols(c if n < 6 else 1 - c, yrel(from_y))]
        remote(dst, dst, y_send.at[k * 10 + n], y_recv.at[k * 10 + n], dev(z, x, y, 1 - c)).wait_recv()

    own_copy = pltpu.make_async_copy(hid.at[:, quarter], raw.at[0, :, own_cols], loc_sem.at[0])

    def y_begin(k):
        if k:
            remote(raw.at[k, :, own_cols], raw.at[k, :, own_cols], xa_send.at[4 - k], xa_recv.at[4 - k],
                   dev(z, xrel(1), y, c)).wait_recv()
        for n in (0, 2, 1, 3, 6):
            go(y_copy(k, n))

    def y_middle(k, n):
        y_wait(k, 2 * n)
        go(y_copy(k, 4 + n))

    def y_side(k, n):
        y_wait(k, 2 * n + 1)
        go(y_copy(k, 7 + n))

    def y_end(k):
        for n in (4, 5):
            y_wait(k, n)
        go(y_copy(k, 9))

    def y_done(k):
        for n in (6, 7, 8, 9):
            y_wait(k, n)
        norm(k)

    def x_begin():
        for d in (2, 1, 3):
            go(xa(d))
        own_copy.start()

    def xu(d):
        return remote(xus.at[d], xur.at[d], xu_send.at[d], xu_recv.at[d], dev(z, xrel(d), y, c))

    def up_begin(k):
        row = lax.broadcasted_iota(jnp.int32, (128, 128), 0)
        rank = lax.broadcasted_iota(jnp.int32, (128, 128), 1) & 15
        hit = (avb[k, 9:10, 0:128] == (4 * (row >> 4) + x).astype(F32)) & ((row & 15) == rank)
        choice = jnp.where(hit, 1.0, 0.0).T[0:64].astype(BF)
        xus[k] = jnp.dot(choice, ug[...], preferred_element_type=F32).astype(BF)
        if k:
            go(xu(k))

    def up_end():
        total = xus[0].astype(F32)
        for d in (1, 2, 3):
            xu(d).wait_recv()
            total = total + xur[d].astype(F32)
        usel[...] = total.astype(BF)

    def lrx(k):
        return remote(lrx_s.at[k], lrx_r.at[k], lr_send.at[k], lr_recv.at[k], dev(z, xrel(k), y, c))

    def low_partial(k):
        part = lax.dot_general(
            dg[...].reshape(NZ * 48, 1024), act[k, :, pl.ds(mo(c * 1024, 1024), 1024)],
            (((1,), (1,)), ((), ())), preferred_element_type=F32)
        ids = avb[k, 8:9, :]
        out = None
        for q in range(NZ):
            hit = ids == (4 * q + y).astype(F32)
            term = jnp.where(hit, part[q * 48:(q + 1) * 48, :], 0.0)
            out = term if out is None else out + term
        lrx_s[k] = out
        if k:
            go(lrx(k))

    def low_core():
        total = lrx_s[0]
        for k in range(1, 4):
            lrx(k).wait_recv()
            total = total + lrx_r[k]
        lrc_s[...] = total
        go(remote(lrc_s, lrc_r, lr_send.at[4], lr_recv.at[4], dev(z, x, y, 1 - c)))

    def lry(d):
        return remote(lry_s, lry_r.at[d], lr_send.at[4 + d], lr_recv.at[4 + d], dev(z, x, yrel(d), c))

    def low_y():
        remote(lrc_s, lrc_r, lr_send.at[4], lr_recv.at[4], dev(z, x, y, 1 - c)).wait_recv()
        lry_s[...] = lrc_s[...] + lrc_r[...]
        for d in range(1, 4):
            go(lry(d))

    def low_end():
        total = lry_s[...]
        for d in range(1, 4):
            lry(d).wait_recv()
            total = total + lry_r[d]
        low = total.astype(BF)
        row = lax.broadcasted_iota(jnp.int32, (64, RANK), 0)
        rank = lax.broadcasted_iota(jnp.int32, (64, RANK), 1)
        repeat = ((row & 15) == rank).astype(BF)
        hit = (lax.broadcasted_iota(jnp.int32, (64, T), 0) >> 4) == pick(
            lax.broadcasted_iota(jnp.int32, (64, T), 1), 0, 1, 2, 3)
        for j in range(3):
            spread = jnp.dot(repeat, low[j * RANK:(j + 1) * RANK, :], preferred_element_type=F32)
            lhs[j] = jnp.where(hit, spread, 0.0).T.astype(BF)

    def make_bias():
        tc = lax.broadcasted_iota(jnp.int32, (T, T), 0)
        tr = lax.broadcasted_iota(jnp.int32, (T, T), 1)
        allowed = (pick(tc, 0, 1, 2, 3) == pick(tr, 0, 1, 2, 3)) & (tr <= tc)
        bias[...] = jnp.where(allowed, 0.0, -1e30)

    def part(k, j):
        return jnp.dot(act[k], wg[j][...], preferred_element_type=F32)

    def relay(j, d):
        return remote(relay_s[j].at[d], relay_r[j].at[d], rs_send.at[j * 4 + d], rs_recv.at[j * 4 + d],
                      dev(z, xrel(1 - 2 * d), y, c))

    def final(j, d):
        return remote(fin_s[j].at[d], fin_r[j].at[d], rs_send.at[j * 4 + 2 + d], rs_recv.at[j * 4 + 2 + d],
                      dev(z, xrel(1 - 2 * d), y, c))

    def rs_far(j):
        p = part(2, j).astype(BF)
        for d in (0, 1):
            relay_s[j][d] = p[d * 192:(d + 1) * 192]
            go(relay(j, d))

    def rs_near(j, d):
        p = part(1 if d == 0 else 3, j)
        relay(j, d).wait_recv()
        lo = d * 192
        fin_s[j][d, lo:lo + 192] = (p[lo:lo + 192] + relay_r[j][d].astype(F32)).astype(BF)
        fin_s[j][d, 192 - lo:384 - lo] = p[192 - lo:384 - lo].astype(BF)
        go(final(j, d))

    def rs_own(j):
        own[j][...] = part(0, j)

    def rotate(v):
        return v * cosb[...] + pltpu.roll(v, HEAD // 2, axis=1) * sinb[...]

    def chunk_end(j, i):
        if i == 0:
            for d in (0, 1):
                final(j, d).wait_recv()
        cols = slice(i * 128, (i + 1) * 128) if j else slice(0, 256)
        base = own[j][:, cols]
        for d in (0, 1):
            base = base + fin_r[j][d, :, cols].astype(F32)
        if j == 0:
            k = base[:, 0:128] + ADAPTER_SCALE * jnp.dot(lhs[1], usel[:, 0:128], preferred_element_type=F32)
            v = base[:, 128:256] + ADAPTER_SCALE * jnp.dot(lhs[2], usel[:, 128:256], preferred_element_type=F32)
            k, v = rotate(k).astype(BF), v.astype(BF)
            keys[...] = k
            vals[...] = v
            key_o[...] = k
            val_o[...] = v
            return
        lo = STARTS[j] + i * 128
        base = base + ADAPTER_SCALE * jnp.dot(lhs[0], usel[:, lo:lo + 128], preferred_element_type=F32)
        q = rotate(base).astype(BF)
        for n in range(3):
            rows, wide = slice(n * 128, (n + 1) * 128), (n + 1) * 128
            s = lax.dot_general(q[rows], keys[0:wide, :], (((1,), (1,)), ((), ())), preferred_element_type=F32)
            s = s * (1.0 / math.sqrt(HEAD)) + bias[rows, 0:wide]
            e = jnp.exp(s - jnp.max(s, axis=1, keepdims=True))
            a = (e / jnp.sum(e, axis=1, keepdims=True)).astype(BF)
            o = jnp.dot(a, vals[0:wide, :], preferred_element_type=F32)
            ctx_o[rows, lo - 256:lo - 128] = o.astype(BF)

    steps = {
        "begin": begin, "tables": tables, "fac": factors, "sw": sides, "uw": up_end, "bias": make_bias,
        "zs": z_start, "zw": z_step, "xs": x_begin, "yb": y_begin, "ym": y_middle, "ys": y_side, "ye": y_end, "yd": y_done,
        "up": up_begin, "lp": low_partial, "lc": low_core, "ly": low_y, "le": low_end,
        "far": rs_far, "near": rs_near, "own": rs_own, "end": chunk_end,
    }
    for name, *arguments in ORDER:
        steps[name](*arguments)

    for copy in sent:
        copy.wait_send()

    @pl.when(y != x)
    def _():
        remote(down.at[:, pl.ds(mo(x * 256, 256), 256)], dg.at[z, :, pl.ds(mo(y * 256, 256), 256)],
               d1_send.at[0], d1_recv.at[y], dev(z, x, x, c)).wait_send()


def hand_over(ctx, key, val, ctx_o, key_o, val_o):
    ctx_o[...] = ctx[...]
    key_o[...] = key[...]
    val_o[...] = val[...]


def shards(hidden, gain, qw, kvw, down, up_q, up_kv, lens, picks):
    half = np.arange(HEAD // 2, dtype=np.float32) * np.float32(2.0) / np.float32(HEAD)
    one = np.power(np.float32(ROPE_BASE), -half).astype(np.float32)
    freq = jnp.asarray(np.tile(np.concatenate([one, one])[None, :], (8, 1)))
    vmem, smem = pl.BlockSpec(memory_space=pltpu.VMEM), pl.BlockSpec(memory_space=pltpu.SMEM)
    dma = pltpu.SemaphoreType.DMA
    scratch = [
        [pltpu.VMEM((2048, w), BF) for w in WIDTHS],
        pltpu.VMEM((4, T, 2048), BF),
        pltpu.VMEM((4, T, 2048), BF),
        pltpu.VMEM((8, 48, 1024), BF),
        pltpu.VMEM((128, 1280), BF),
        pltpu.VMEM((8, 8, T), F32),
        pltpu.VMEM((4, 16, T), F32),
        pltpu.VMEM((8, 2048), F32),
        [pltpu.VMEM((2, 192, w), BF) for w in WIDTHS],
        [pltpu.VMEM((2, 192, w), BF) for w in WIDTHS],
        [pltpu.VMEM((2, T, w), BF) for w in WIDTHS],
        [pltpu.VMEM((2, T, w), BF) for w in WIDTHS],
        [pltpu.VMEM((T, w), F32) for w in WIDTHS],
        pltpu.VMEM((4, 48, T), F32),
        pltpu.VMEM((4, 48, T), F32),
        pltpu.VMEM((48, T), F32),
        pltpu.VMEM((48, T), F32),
        pltpu.VMEM((48, T), F32),
        pltpu.VMEM((4, 48, T), F32),
        pltpu.VMEM((3, T, 64), BF),
        pltpu.VMEM((T, T), F32),
        pltpu.VMEM((T, HEAD), F32),
        pltpu.VMEM((T, HEAD), F32),
        pltpu.VMEM((T, HEAD), BF),
        pltpu.VMEM((T, HEAD), BF),
        pltpu.VMEM((4, 64, 1280), BF),
        pltpu.VMEM((4, 64, 1280), BF),
        pltpu.VMEM((64, 1280), BF),
        dma((8 * len(ITEMS),)), dma((8 * len(ITEMS),)),
        dma((40,)), dma((40,)),
        dma((4,)), dma((4,)),
        dma((4,)), dma((4,)),
        dma((4,)), dma((4,)),
        dma((8,)), dma((8,)),
        dma((4,)), dma((4,)),
        dma((4 * CHUNKS,)), dma((4 * CHUNKS,)),
        dma((8,)), dma((8,)),
        dma((1,)),
    ]
    context, keys, values = pl.pallas_call(
        kernel,
        out_shape=(
            jax.ShapeDtypeStruct((T, 1024), BF),
            jax.ShapeDtypeStruct((T, HEAD), BF),
            jax.ShapeDtypeStruct((T, HEAD), BF),
        ),
        in_specs=[vmem] * 8 + [smem] * 2,
        out_specs=(vmem, vmem, vmem),
        scratch_shapes=scratch,
        compiler_params=pltpu.CompilerParams(
            collective_id=0, has_side_effects=True, vmem_limit_bytes=56 * 1024 * 1024
        ),
        cost_estimate=pl.CostEstimate(flops=10_000_000_000, bytes_accessed=4_000_000, transcendentals=1_500_000),
    )(
        hidden, gain.reshape(64, 128), qw, kvw, down.reshape(48, 1024),
        up_q.reshape(16, 1024), up_kv.reshape(16, 256), freq, lens, picks,
    )
    shapes = tuple(jax.ShapeDtypeStruct(a.shape, a.dtype) for a in (context, keys, values))
    return pl.pallas_call(
        hand_over, out_shape=shapes, in_specs=[vmem] * 3, out_specs=(vmem,) * 3,
    )(context, keys, values)


def solution(mesh):
    in_specs = (
        P("req", "blk"), P(), P("req", "blk"), P("req", "blk"), P("req", None, None, "blk"),
        P("req", None, "blk"), P("req", None, "blk"), P("req", None), P("req", None),
    )
    out_specs = (P("req", "blk"), P("req", "blk"), P("req", "blk"))
    return jax.shard_map(shards, mesh=mesh, in_specs=in_specs, out_specs=out_specs, check_vma=False)
```

time: 120 us -> 105 us (0.88)
  Pallas kernels: 116 us -> 104 us
  local copies, waits for them, and re-layouts: 3.67 us -> 0 us
    pallas_call x1, Pallas kernels: 116 us -> 102 us  [shards(): pl.pallas_call(kernel, out_shape=(jax.ShapeDtypeStruct((T, 1024), BF), ja...]
    unnamed x7 -> x0, local copies, waits for them, and re-layouts: 3.67 us -> none
    pallas_call x0 -> x1, Pallas kernels: none -> 2.15 us  [shards(): pl.pallas_call(hand_over, out_shape=shapes, in_specs=[vmem] * 3, out_spec...]
where the time goes in v2:
time: 105 us
  Pallas kernels  104 us (99%)
    pallas_call x1, Pallas kernels, shards(): pl.pallas_call(kernel, out_shape=(jax.ShapeDtypeStruct((T, 1024), BF), ja...  102 us
    pallas_call x1, Pallas kernels, shards(): pl.pallas_call(hand_over, out_shape=shapes, in_specs=[vmem] * 3, out_spec...  2.15 us

profile of v2, /device:TPU:6, one launch (start us, length us, event | category | flops | bytes accessed | tf_op | source)
XLA Modules:
  0.0 104.5 jit_solution(2069370572506682631)
XLA Ops:
  0.6 101.7 %shard_map.121 = (bf16[384,1024]{1,0:T(8,128)(2,1)}, bf16[384,128]{1,0:T(8,128)(2,1)}, bf16[384,128]{1,0:T(8,128)(2,1)}) custom-call(bf16[384,1024]{1,0:T(8,128)(2,1)} %hid.1, f32[64,128]{1,0:T(8,128)} %bitcast.5, bf16[256,1024]{1,0:T(8,128)(2,1)} %qw.1, bf16[256,256]{1,0:T(8,128)(2,1)} %kvw.1, bf16[48,1024]{1,0:T(8,128)(2,1)} %bitcast.4, ...), custom_call_target="tpu_custom_call" | custom-call | flops 10000000000 | bytes 4000000 | tf_op jit(solution)/shard_map/pallas_call | solution.py:497
  102.4 2.2 %shard_map.122 = (bf16[384,1024]{1,0:T(8,128)(2,1)}, bf16[384,128]{1,0:T(8,128)(2,1)}, bf16[384,128]{1,0:T(8,128)(2,1)}) custom-call(bf16[384,1024]{1,0:T(8,128)(2,1)} %get-tuple-element.6.ctx, bf16[384,128]{1,0:T(8,128)(2,1)} %get-tuple-element.7.key, bf16[384,128]{1,0:T(8,128)(2,1)} %get-tuple-element.8.val), custom_call_target="tpu_custom_call" | custom-call | tf_op jit(solution)/shard_map/pallas_call | solution.py:516

commit v3 on v2

--- a/solution.py
+++ b/solution.py
@@ -25,29 +25,29 @@
 ITEMS = ("U", "D") + tuple(range(CHUNKS))
 
 ORDER = (
-    ("begin",), ("yb", 0), ("xs",), ("zs", 0), ("zs", 1), ("tables",), ("bias",), ("fac",), ("zw", 0, 0, 1),
-    ("ym", 0, 0), ("ym", 0, 1), ("zw", 0, 1, 1), ("zs", "U"), ("ys", 0, 0), ("ys", 0, 1), ("zw", 1, 0, 1), ("yb", 2),
-    ("zw", 1, 1, 1), ("sw",), ("ye", 0), ("zw", 0, 0, 2), ("yd", 0), ("yb", 1), ("zw", 0, 1, 2), ("zw", "U", 0, 1),
-    ("ym", 2, 0), ("ym", 2, 1), ("zw", "U", 1, 1), ("yb", 3), ("zw", 1, 0, 2), ("ys", 2, 0), ("ys", 2, 1),
-    ("zw", 1, 1, 2), ("ym", 1, 0), ("ym", 1, 1), ("zw", 0, 0, 3), ("zw", 0, 1, 3), ("zw", "U", 0, 2), ("ys", 1, 0),
-    ("ys", 1, 1), ("zw", "U", 1, 2), ("zs", "D"), ("zw", 1, 0, 3), ("ye", 2), ("zw", 1, 1, 3), ("zs", 2), ("yd", 2),
-    ("ym", 3, 0), ("ym", 3, 1), ("zw", 0, 0, 4), ("far", 0), ("zw", "U", 0, 3), ("own", 0), ("zw", "U", 1, 3),
-    ("zs", 3), ("ys", 3, 0), ("ys", 3, 1), ("zw", "D", 0, 1), ("zw", "D", 1, 1), ("zs", 5), ("ye", 1),
-    ("zw", 1, 0, 4), ("far", 1), ("own", 1), ("zw", 2, 0, 1), ("yd", 1), ("zw", 2, 1, 1), ("ye", 3), ("near", 0, 0),
-    ("zw", "U", 0, 4), ("up", 1), ("up", 2), ("zw", 3, 0, 1), ("up", 3), ("yd", 3), ("zw", 3, 1, 1), ("near", 0, 1),
-    ("up", 0), ("zw", "D", 0, 2), ("near", 1, 0), ("near", 1, 1), ("zw", "D", 1, 2), ("zw", 5, 0, 1), ("zw", 5, 1, 1),
-    ("zw", 2, 0, 2), ("zw", 2, 1, 2), ("zw", 3, 0, 2), ("zw", 3, 1, 2), ("zw", "D", 0, 3), ("zw", "D", 1, 3),
-    ("zw", 5, 0, 2), ("zw", 5, 1, 2), ("zs", 6), ("zw", 2, 0, 3), ("zw", 2, 1, 3), ("zw", 3, 0, 3), ("zw", 3, 1, 3),
-    ("uw",), ("zw", "D", 0, 4), ("zs", 4), ("lp", 0), ("lp", 1), ("lp", 2), ("zw", 5, 0, 3), ("lp", 3),
-    ("zw", 5, 1, 3), ("zw", 6, 0, 1), ("zw", 6, 1, 1), ("zs", 7), ("zw", 2, 0, 4), ("far", 2), ("own", 2),
-    ("zw", 3, 0, 4), ("far", 3), ("own", 3), ("zw", 4, 0, 1), ("zw", 4, 1, 1), ("zw", 5, 0, 4), ("far", 5),
-    ("own", 5), ("lc",), ("zw", 6, 0, 2), ("near", 2, 0), ("zw", 6, 1, 2), ("near", 2, 1), ("ly",), ("zw", 7, 0, 1),
-    ("near", 3, 0), ("near", 3, 1), ("zw", 7, 1, 1), ("near", 5, 0), ("zw", 4, 0, 2), ("near", 5, 1), ("zw", 4, 1, 2),
-    ("zw", 6, 0, 3), ("zw", 6, 1, 3), ("zw", 7, 0, 2), ("zw", 7, 1, 2), ("zw", 4, 0, 3), ("le",), ("zw", 4, 1, 3),
-    ("end", 0, 0), ("zw", 6, 0, 4), ("far", 6), ("zw", 7, 0, 3), ("own", 6), ("end", 1, 0), ("zw", 4, 0, 4),
-    ("zw", 7, 1, 3), ("far", 4), ("own", 4), ("end", 1, 1), ("zw", 7, 0, 4), ("near", 6, 0), ("near", 6, 1),
-    ("far", 7), ("own", 7), ("end", 2, 0), ("near", 4, 0), ("near", 4, 1), ("end", 3, 0), ("end", 5, 0),
-    ("near", 7, 0), ("near", 7, 1), ("end", 6, 0), ("end", 4, 0), ("end", 7, 0),
+    ("begin",), ("yb", 0), ("xs",), ("zs", "U"), ("zs", 0), ("tables",), ("bias",), ("zw", "U", 0, 1),
+    ("zw", "U", 1, 1), ("fac",), ("zs", 1), ("ym", 0, 0), ("ym", 0, 1), ("zw", 0, 0, 1), ("zw", 0, 1, 1), ("zs", 2),
+    ("ys", 0, 0), ("ys", 0, 1), ("zw", "U", 0, 2), ("zw", "U", 1, 2), ("yb", 2), ("sw",), ("zw", 1, 0, 1), ("ye", 0),
+    ("zw", 1, 1, 1), ("yd", 0), ("zw", 0, 0, 2), ("ym", 2, 0), ("ym", 2, 1), ("yb", 1), ("zw", 0, 1, 2),
+    ("zw", 2, 0, 1), ("ys", 2, 0), ("ys", 2, 1), ("zw", 2, 1, 1), ("zw", "U", 0, 3), ("zw", "U", 1, 3), ("ye", 2),
+    ("zw", 1, 0, 2), ("yd", 2), ("zw", 1, 1, 2), ("zs", 3), ("ym", 1, 0), ("ym", 1, 1), ("yb", 3), ("zw", 0, 0, 3),
+    ("ys", 1, 0), ("ys", 1, 1), ("zw", 0, 1, 3), ("zw", 2, 0, 2), ("zw", 2, 1, 2), ("zs", "D"), ("zw", "U", 0, 4),
+    ("up", 1), ("up", 2), ("ye", 1), ("up", 3), ("up", 0), ("zw", 1, 0, 3), ("yd", 1), ("ym", 3, 0), ("ym", 3, 1),
+    ("zw", 1, 1, 3), ("zw", 3, 0, 1), ("zw", 3, 1, 1), ("ys", 3, 0), ("ys", 3, 1), ("zw", 0, 0, 4), ("far", 0),
+    ("own", 0), ("zw", 2, 0, 3), ("ye", 3), ("zw", 2, 1, 3), ("zw", "D", 0, 1), ("yd", 3), ("zw", "D", 1, 1), ("uw",),
+    ("zw", 1, 0, 4), ("zs", 4), ("far", 1), ("zw", 3, 0, 2), ("own", 1), ("near", 0, 0), ("zw", 3, 1, 2),
+    ("near", 0, 1), ("zw", 2, 0, 4), ("far", 2), ("own", 2), ("zw", "D", 0, 2), ("zw", "D", 1, 2), ("zs", 6),
+    ("zw", 4, 0, 1), ("near", 1, 0), ("zw", 4, 1, 1), ("near", 1, 1), ("zw", 3, 0, 3), ("zw", 3, 1, 3),
+    ("zw", "D", 0, 3), ("zw", "D", 1, 3), ("zw", 6, 0, 1), ("near", 2, 0), ("zw", 6, 1, 1), ("near", 2, 1),
+    ("zw", 4, 0, 2), ("zw", 4, 1, 2), ("zw", 3, 0, 4), ("far", 3), ("own", 3), ("zw", "D", 0, 4), ("zs", 7),
+    ("lp", 0), ("lp", 1), ("zw", 6, 0, 2), ("lp", 2), ("lp", 3), ("zw", 6, 1, 2), ("zw", 4, 0, 3), ("zw", 4, 1, 3),
+    ("zs", 5), ("zw", 7, 0, 1), ("near", 3, 0), ("zw", 7, 1, 1), ("near", 3, 1), ("zw", 6, 0, 3), ("zw", 6, 1, 3),
+    ("zw", 4, 0, 4), ("far", 4), ("own", 4), ("zw", 5, 0, 1), ("lc",), ("zw", 5, 1, 1), ("zw", 7, 0, 2), ("ly",),
+    ("zw", 7, 1, 2), ("zw", 6, 0, 4), ("far", 6), ("near", 4, 0), ("zw", 5, 0, 2), ("near", 4, 1), ("zw", 5, 1, 2),
+    ("own", 6), ("zw", 7, 0, 3), ("zw", 7, 1, 3), ("near", 6, 0), ("zw", 5, 0, 3), ("near", 6, 1), ("zw", 5, 1, 3),
+    ("le",), ("zw", 7, 0, 4), ("far", 7), ("end", 0, 0), ("own", 7), ("zw", 5, 0, 4), ("far", 5), ("own", 5),
+    ("end", 1, 0), ("end", 1, 1), ("near", 7, 0), ("near", 7, 1), ("near", 5, 0), ("near", 5, 1), ("end", 2, 0),
+    ("end", 3, 0), ("end", 4, 0), ("end", 6, 0), ("end", 7, 0), ("end", 5, 0),
 )
 
 
@@ -420,7 +420,7 @@
             s = lax.dot_general(q[rows], keys[0:wide, :], (((1,), (1,)), ((), ())), preferred_element_type=F32)
             s = s * (1.0 / math.sqrt(HEAD)) + bias[rows, 0:wide]
             e = jnp.exp(s - jnp.max(s, axis=1, keepdims=True))
-            a = (e / jnp.sum(e, axis=1, keepdims=True)).astype(BF)
+            a = (e * (1.0 / jnp.sum(e, axis=1, keepdims=True))).astype(BF)
             o = jnp.dot(a, vals[0:wide, :], preferred_element_type=F32)
             ctx_o[rows, lo - 256:lo - 128] = o.astype(BF)
 

time: 105 us -> 102 us (0.971); the launches traced: 105 us -> 99.9 us
  Pallas kernels: 104 us -> 99.3 us
    pallas_call x1, Pallas kernels: 102 us -> 97.2 us  [shards(): pl.pallas_call(kernel, out_shape=(jax.ShapeDtypeStruct((T, 1024), BF), ja...]
where the time goes in v3:
time: 102 us; the launch traced here: 99.9 us
  Pallas kernels  99.3 us (97%)
    pallas_call x1, Pallas kernels, shards(): pl.pallas_call(kernel, out_shape=(jax.ShapeDtypeStruct((T, 1024), BF), ja...  97.2 us
    pallas_call x1, Pallas kernels, shards(): pl.pallas_call(hand_over, out_shape=shapes, in_specs=[vmem] * 3, out_spec...  2.15 us

profile of v3, /device:TPU:6, one launch (start us, length us, event | category | flops | bytes accessed | tf_op | source)
XLA Modules:
  0.0 99.9 jit_solution(15181359549285811301)
XLA Ops:
  0.6 97.2 %shard_map.121 = (bf16[384,1024]{1,0:T(8,128)(2,1)}, bf16[384,128]{1,0:T(8,128)(2,1)}, bf16[384,128]{1,0:T(8,128)(2,1)}) custom-call(bf16[384,1024]{1,0:T(8,128)(2,1)} %hid.1, f32[64,128]{1,0:T(8,128)} %bitcast.5, bf16[256,1024]{1,0:T(8,128)(2,1)} %qw.1, bf16[256,256]{1,0:T(8,128)(2,1)} %kvw.1, bf16[48,1024]{1,0:T(8,128)(2,1)} %bitcast.4, ...), custom_call_target="tpu_custom_call" | custom-call | flops 10000000000 | bytes 4000000 | tf_op jit(solution)/shard_map/pallas_call | solution.py:497
  97.8 2.2 %shard_map.122 = (bf16[384,1024]{1,0:T(8,128)(2,1)}, bf16[384,128]{1,0:T(8,128)(2,1)}, bf16[384,128]{1,0:T(8,128)(2,1)}) custom-call(bf16[384,1024]{1,0:T(8,128)(2,1)} %get-tuple-element.6.ctx, bf16[384,128]{1,0:T(8,128)(2,1)} %get-tuple-element.7.key, bf16[384,128]{1,0:T(8,128)(2,1)} %get-tuple-element.8.val), custom_call_target="tpu_custom_call" | custom-call | tf_op jit(solution)/shard_map/pallas_call | solution.py:516
